TPU v7x, 256 devices: a whole 4x4x8 slice. The times are simulated.
256 devices in a mesh: wa: 8 (over z), vert: 32 (over y, x, core).
Axes of the slice: x: 4, y: 4, z: 8, core: 2. Of those that a mesh axis runs over, the one named last changes fastest.
Arguments:
- hidden_in: bfloat16 [384, 8192], P(None, 'wa')
- gate_levels: bfloat16 [8192, 28672], P('wa', 'vert'), may hold values from -127 to 127, as said below
- up_levels: bfloat16 [8192, 28672], P('wa', 'vert'), may hold values from -127 to 127, as said below
- gate_scale: float32 [28672], P('vert'), as said below
- up_scale: float32 [28672], P('vert'), as said below
- down_levels: bfloat16 [28672, 8192], P('vert', 'wa'), may hold values from -127 to 127, as said below
- down_scale: float32 [8192], P('wa'), as said below
- norm_gain: float32 [8192], P('wa'), may hold values from 0.5 to 1.5
- head_weight: bfloat16 [8192, 16000], P('wa', 'vert')
- reward_states: bfloat16 [8, 384, 4096], P('wa', None, 'vert'), may hold values from -6 to 6
- reward_gain: float32 [8, 4096], P('wa'), may hold values from 0.5 to 1.5
- reward_heads: bfloat16 [8, 4096, 16000], P('wa', None, 'vert')
- preference: int32 [384, 8], P(None, 'wa'), may hold values from 0 to 16
- token_ids: int32 [384], P('wa'), may hold values from 0 to 15999
Outputs:
- log_probs: float32 [384, 16000], P('wa', 'vert')
- chosen: float32 [384], P('wa')
Inputs may be any that keep to these rules, and one draw needn't show every extreme that they name: `gate_levels`: whole numbers. `up_levels`: whole numbers. `down_levels`: whole numbers. `gate_scale`: positive. `up_scale`: positive. `down_scale`: positive.
All inputs are finite; a program needn't handle non-finite values.
Results may differ from a plain program's by a relative error of at most 0.0025.
Values may be sent and summed in bfloat16 or wider, within the bound.
No kernel may reach another device: no remote copies, remote signals or barrier semaphores. Data moves between devices by JAX's collectives and lax.ppermute only.
A program may use at most 64 MiB of HBM per device.

v0:
```python
import jax
import jax.numpy as jnp
from jax import lax
from jax.sharding import PartitionSpec as P

D = 8192


def log_total(values):
    local_top = jnp.max(values, axis=-1)
    top = lax.pmax(local_top, "vert")
    total = lax.psum(jnp.sum(jnp.exp(values - top[..., None]), axis=-1), "vert")
    return top + jnp.log(total)


def normalize(resid, norm_gain):
    squares = lax.psum(jnp.sum(resid * resid, axis=1), "wa")
    return (resid * lax.rsqrt(squares[:, None] / D + 1e-05) * norm_gain).astype(jnp.bfloat16)


def local(
    hidden_in,
    gate_levels,
    up_levels,
    gate_scale,
    up_scale,
    down_levels,
    down_scale,
    norm_gain,
    head_weight,
    reward_states,
    reward_gain,
    reward_heads,
    preference,
    token_ids,
):
    gate_part = jnp.dot(hidden_in, gate_levels, preferred_element_type=jnp.float32)
    up_part = jnp.dot(hidden_in, up_levels, preferred_element_type=jnp.float32)
    gate, up = lax.psum((gate_part, up_part), "wa")
    hidden = (jax.nn.silu(gate * gate_scale) * (up * up_scale)).astype(jnp.bfloat16)
    down_part = jnp.dot(hidden, down_levels, preferred_element_type=jnp.float32)
    down = lax.psum(down_part, "vert") * down_scale
    resid = hidden_in.astype(jnp.float32) + down
    normed = normalize(resid, norm_gain)
    base_part = jnp.dot(normed, head_weight, preferred_element_type=jnp.float32)
    states = lax.all_gather(reward_states, "vert", axis=2, tiled=True)
    state_values = states.astype(jnp.float32)
    state_scale = lax.rsqrt(jnp.mean(state_values * state_values, axis=2, keepdims=True) + 1e-05)
    reward_normed = (state_values * state_scale * reward_gain[:, None, :]).astype(jnp.bfloat16)
    reward_logits = jnp.einsum(
        "rnd,rdv->rnv", reward_normed, reward_heads, preferred_element_type=jnp.float32
    )
    reward_logp = reward_logits - log_total(reward_logits)[..., None]
    weights = preference.astype(jnp.float32).T / 16.0
    weighted = jnp.sum(weights[:, :, None] * reward_logp, axis=0)
    base_rows, reward_rows = (
        lax.psum_scatter(base_part, "wa", scatter_dimension=0, tiled=True),
        lax.psum_scatter(weighted, "wa", scatter_dimension=0, tiled=True),
    )
    base_logp = base_rows - log_total(base_rows)[:, None]
    mix = base_logp + reward_rows
    log_probs = mix - log_total(mix)[:, None]
    columns = log_probs.shape[1]
    vocab_index = lax.axis_index("vert") * columns + lax.iota(jnp.int32, columns)
    picked = jnp.sum(jnp.where(vocab_index[None, :] == token_ids[:, None], log_probs, 0.0), axis=1)
    chosen = lax.psum(picked, "vert")
    return (log_probs, chosen)


def solution(mesh):
    return jax.shard_map(
        local,
        mesh=mesh,
        in_specs=(
            P(None, "wa"),
            P("wa", "vert"),
            P("wa", "vert"),
            P("vert"),
            P("vert"),
            P("vert", "wa"),
            P("wa"),
            P("wa"),
            P("wa", "vert"),
            P("wa", None, "vert"),
            P("wa", None),
            P("wa", None, "vert"),
            P(None, "wa"),
            P("wa"),
        ),
        out_specs=(P("wa", "vert"), P("wa")),
        check_vma=False,
    )
```

profile of v0, /device:TPU:1, one launch (start us, length us, event | category | flops | bytes accessed | tf_op | source)
XLA Modules:
  0.0 702.5 jit_solution(15787238454085852242)
XLA Ops:
  7.2 0.0 copy-start
  7.2 0.0 copy-start.3
  7.2 0.0 all-reduce.8.cloned.1.call-start
  7.2 3.9 fusion.17
  11.2 0.0 copy-done.3
  11.2 2.0 fusion.18
  13.2 0.0 all-reduce.8.cloned.1.call-update
  13.3 0.0 all-reduce.6.cloned.1.call-start
  13.3 89.1 %all-reduce.8.cloned.1.call-done = (f32[384,896]{1,0:T(8,128)}, f32[384,896]{1,0:T(8,128)}) async-done(((f32[384,896]{1,0:T(8,128)}, f32[384,896]{1,0:T(8,128)}), (f32[384,896]{1,0:T(8,128)}, f32[384,896]{1,0:T(8,128)})) %all-reduce.8.cloned.1.call-update) | async-done | bytes 2752528 | tf_op jit(solution)/shard_map/psum | solution.py:39
  102.5 0.0 copy-done.12
  102.5 3.9 fusion.13
  106.4 0.0 all-reduce.6.cloned.1.call-update
  106.4 0.0 copy-start.7
  106.5 0.0 reduce-scatter.7.cloned.1.call-start
  106.5 116.9 %all-reduce.6.cloned.1.call-done = f32[384,1024]{1,0:T(8,128)} async-done(((f32[384,1024]{1,0:T(8,128)}), f32[384,1024]{1,0:T(8,128)}) %all-reduce.6.cloned.1.call-update) | async-done | bytes 1572880 | tf_op jit(solution)/shard_map/psum | solution.py:42
  223.4 2.1 multiply_reduce_fusion
  225.4 13.7 %psum.59 = f32[384]{0:T(512)S(1)} all-reduce(f32[384]{0:T(512)S(1)} %multiply_reduce_fusion), channel_id=1, replica_groups=mesh['wa'=8,'vert'=32] {'wa'}, use_global_device_ids=true, to_apply=%region_4.5 | all-reduce | flops 384 | bytes 3072 | tf_op jit(solution)/shard_map/psum | solution.py:17
  239.1 0.0 copy-start.8
  239.1 3.0 fusion.9
  242.1 0.0 reduce-scatter.7.cloned.1.call-update
  242.1 0.0 all-gather.2.cloned.1.call-start
  242.2 0.5 all-gather.2.cloned.1.call-update
  242.7 0.0 reduce-scatter.9.cloned.1.call-start
  242.8 33.5 %reduce-scatter.7.cloned.1.call-done = f32[48,500]{1,0:T(8,128)} async-done(((f32[384,500]{1,0:T(8,128)}), f32[48,500]{1,0:T(8,128)}) %reduce-scatter.7.cloned.1.call-update) | async-done | bytes 96016
  276.3 1.0 copy.23
  277.4 0.0 copy-start.11
  277.4 1.1 reduce_max.29
  278.5 55.9 %all-gather.2.cloned.1.call-done = bf16[1,384,4096]{2,1,0:T(8,128)(2,1)} async-done(((bf16[1,384,128]{2,1,0:T(8,128)(2,1)}), bf16[1,384,4096]{2,1,0:T(8,128)(2,1)}) %all-gather.2.cloned.1.call-update) | async-done | bytes 3145744 | tf_op jit(solution)/shard_map/all_gather | solution.py:46
  334.3 2.7 fusion
  337.1 0.1 copy-done.2
  337.2 4.6 fusion.16
  341.8 62.3 %all-reduce.1 = (f32[1,384]{1,0:T(1,128)S(1)}, f32[48]{0:T(128)S(1)}) all-reduce(f32[1,384]{1,0:T(1,128)S(1)} %reduce_max.31, f32[48]{0:T(128)S(1)} %reduce_max.29), channel_id=1, replica_groups=mesh['wa'=8,'vert'=32] {'vert'}, use_global_device_ids=true, to_apply=%region_12.13 | all-reduce | flops 432 | bytes 3456 | tf_op jit(solution)/shard_map/pmax | solution.py:11
  404.1 0.2 exponential_reduce_fusion
  404.3 0.1 exponential_reduce_fusion.2
  404.4 65.2 %all-reduce = (f32[1,384]{1,0:T(1,128)S(1)}, f32[48]{0:T(128)S(1)}) all-reduce(f32[1,384]{1,0:T(1,128)S(1)} %reduce_sum.64, f32[48]{0:T(128)S(1)} %exponential_reduce_fusion.2), channel_id=1, replica_groups=mesh['wa'=8,'vert'=32] {'vert'}, use_global_device_ids=true, to_apply=%region_14.15 | all-reduce | flops 432 | bytes 3456 | tf_op jit(solution)/shard_map/psum | solution.py:12
  469.6 0.1 subtract_multiply_fusion
  469.7 0.0 copy-start.9
  469.7 1.2 copy.24
  470.9 0.0 reduce-scatter.9.cloned.1.call-update
  471.0 29.6 %reduce-scatter.9.cloned.1.call-done = f32[48,500]{1,0:T(8,128)} async-done(((f32[384,500]{1,0:T(8,128)}), f32[48,500]{1,0:T(8,128)}) %reduce-scatter.9.cloned.1.call-update) | async-done | bytes 96016
  500.5 1.0 copy.25
  501.6 0.1 fusion.15
  501.7 67.5 %pmax.23 = f32[48]{0:T(128)S(1)} all-reduce(f32[48]{0:T(128)S(1)} %get-tuple-element.14), channel_id=1, replica_groups=mesh['wa'=8,'vert'=32] {'vert'}, use_global_device_ids=true, to_apply=%region_17.18 | all-reduce | flops 48 | bytes 384 | tf_op jit(solution)/shard_map/pmax | solution.py:11
  569.2 0.1 exponential_reduce_fusion.1
  569.3 62.7 %psum.62 = f32[48]{0:T(128)S(1)} all-reduce(f32[48]{0:T(128)S(1)} %exponential_reduce_fusion.1), channel_id=1, replica_groups=mesh['wa'=8,'vert'=32] {'vert'}, use_global_device_ids=true, to_apply=%region_19.20 | all-reduce | flops 48 | bytes 384 | tf_op jit(solution)/shard_map/psum | solution.py:12
  632.0 0.2 select_reduce_fusion
  632.1 0.8 copy.20
  632.9 63.2 %psum.63 = f32[48]{0:T(128)} all-reduce(f32[48]{0:T(128)S(1)} %get-tuple-element.12), channel_id=1, replica_groups=mesh['wa'=8,'vert'=32] {'vert'}, use_global_device_ids=true, to_apply=%region_21.22 | all-reduce | flops 48 | bytes 384 | tf_op jit(solution)/shard_map/psum | solution.py:66
  (29 shorter events, 0.2 us)
Async XLA Ops:
  7.2 95.3 %copy-start = (bf16[896,1024]{1,0:T(8,128)(2,1)S(1)}, bf16[896,1024]{1,0:T(8,128)(2,1)}, u32[]{:S(2)}) copy-start(bf16[896,1024]{1,0:T(8,128)(2,1)} %param.19) | copy-start | bytes 5505028
  7.2 4.0 copy-start.3
  7.2 95.3 %all-reduce.8.cloned.1.call-start = ((), (), s32[]{:S(2)}) async-start(), calls=%async_computation.6 | async-start | bytes 5505024 | tf_op jit(solution)/shard_map/psum | solution.py:39
  7.2 4.0 copy-start.10
  13.2 89.2 %copy-start.12 = (f32[896]{0:T(1024)S(1)}, f32[896]{0:T(1024)}, u32[]{:S(2)}) copy-start(f32[896]{0:T(1024)} %param.18) | copy-start | bytes 10756
  13.2 89.2 %copy-start.13 = (f32[896]{0:T(1024)S(1)}, f32[896]{0:T(1024)}, u32[]{:S(2)}) copy-start(f32[896]{0:T(1024)} %param.17) | copy-start | bytes 10756
  13.3 210.1 %all-reduce.6.cloned.1.call-start = ((), (), s32[]{:S(2)}) async-start(), calls=%async_computation.2 | async-start | bytes 3145728 | tf_op jit(solution)/shard_map/psum | solution.py:42
  106.4 116.9 %copy-start.6 = (f32[1024]{0:T(1024)S(1)}, f32[1024]{0:T(1024)}, u32[]{:S(2)}) copy-start(f32[1024]{0:T(1024)} %param.20) | copy-start | bytes 12292
  106.4 132.7 %copy-start.7 = (f32[1024]{0:T(1024)S(1)}, f32[1024]{0:T(1024)}, u32[]{:S(2)}) copy-start(f32[1024]{0:T(1024)} %param.21) | copy-start | bytes 12292
  106.5 169.9 %reduce-scatter.7.cloned.1.call-start = ((), (), s32[]{:S(2)}) async-start(), calls=%async_computation.4 | async-start | bytes 884736
  223.4 15.8 %copy-start.1 = (f32[384,1024]{1,0:T(8,128)S(1)}, f32[384,1024]{1,0:T(8,128)}, u32[]{:S(2)}) copy-start(f32[384,1024]{1,0:T(8,128)} %all-reduce.6.cloned.1.call-done) | copy-start | bytes 4718596
  239.1 3.6 copy-start.8
  242.1 92.2 %all-gather.2.cloned.1.call-start = ((), (), s32[]{:S(2)}) async-start(), calls=%async_computation.3 | async-start | bytes 3244032 | tf_op jit(solution)/shard_map/all_gather | solution.py:46
  242.7 257.8 %reduce-scatter.9.cloned.1.call-start = ((), (), s32[]{:S(2)}) async-start(), calls=%async_computation.5 | async-start | bytes 884736
  277.3 126.9 %copy-start.4 = (f32[48,500]{0,1:T(8,128)}, f32[48,500]{0,1:T(8,128)S(1)}, u32[]{:S(2)}) copy-start(f32[48,500]{0,1:T(8,128)S(1)} %copy.23) | copy-start | bytes 288004
  277.4 59.7 %copy-start.11 = (f32[1,4096]{1,0:T(1,128)S(1)}, f32[1,4096]{1,0:T(1,128)}, u32[]{:S(2)}) copy-start(f32[1,4096]{1,0:T(1,128)} %param.24) | copy-start | bytes 49156
  334.3 2.8 copy-start.2
  469.7 31.8 %copy-start.5 = (f32[48,500]{0,1:T(8,128)S(1)}, f32[48,500]{0,1:T(8,128)}, u32[]{:S(2)}) copy-start(f32[48,500]{0,1:T(8,128)} %copy-done.4) | copy-start | bytes 288004
  469.7 162.2 %copy-start.9 = (s32[48]{0:T(128)S(1)}, s32[48]{0:T(128)}, u32[]{:S(2)}) copy-start(s32[48]{0:T(128)} %param.27) | copy-start | bytes 580
Sparse Core Ops, SparseCore 0:
  13.4 89.0 all-reduce.7
  106.6 116.7 all-reduce.5
  242.3 34.0 reduce-scatter.6
  279.0 55.3 all-gather.1
  471.1 29.4 reduce-scatter.8
where the time goes:
time: 703 us
  blocking collectives  335 us (48%)
  waiting for transfers between devices  326 us (46%)
  matrix products  17.5 us (2%)
  between operations  13.9 us (2%)
    pmax x2, blocking collectives, log_total(): top = lax.pmax(local_top, 'vert')  130 us
    psum x2, blocking collectives, log_total(): total = lax.psum(jnp.sum(jnp.exp(values - top[..., None]), axis=-1), 'vert')  128 us
    psum x1, waiting for transfers between devices, local(): down = lax.psum(down_part, 'vert') * down_scale  117 us
    psum x1, waiting for transfers between devices, local(): gate, up = lax.psum((gate_part, up_part), 'wa')  89.1 us
    unnamed x7, waiting for transfers between devices  63.7 us
    psum x1, blocking collectives, local(): chosen = lax.psum(picked, 'vert')  63.2 us
    all_gather x1, waiting for transfers between devices, local(): states = lax.all_gather(reward_states, 'vert', axis=2, tiled=True)  55.9 us
  transfers between devices with their start and end apart: 5, of which 5 were waited for; matrix products, arithmetic and copies ran while one was open for 0% of the time, Pallas kernels for 0%

commit v1 on v0

--- a/solution.py
+++ b/solution.py
@@ -63,7 +63,9 @@
     columns = log_probs.shape[1]
     vocab_index = lax.axis_index("vert") * columns + lax.iota(jnp.int32, columns)
     picked = jnp.sum(jnp.where(vocab_index[None, :] == token_ids[:, None], log_probs, 0.0), axis=1)
-    chosen = lax.psum(picked, "vert")
+    chosen = picked
+    for hop in (1, 2, 4, 8, 16):
+        chosen = chosen + lax.ppermute(chosen, "vert", [(dev, dev ^ hop) for dev in range(32)])
     return (log_probs, chosen)
 
 

time: 703 us -> 656 us (0.933)
  blocking collectives: 335 us -> 271 us
  waiting for transfers between devices: 326 us -> 338 us
    psum x1 -> x0, blocking collectives: 63.2 us -> none  [local(): chosen = lax.psum(picked, 'vert')]
    ppermute x0 -> x5, waiting for transfers between devices: none -> 12.6 us  [local(): lax.ppermute(chosen, 'vert', [(dev, dev ^ hop) for dev in range(32)])]
  transfers between devices with their start and end apart: 5 -> 10, of which waited for: 5 -> 10; matrix products, arithmetic and copies ran while one was open for 0% -> 0% of each run, Pallas kernels for 0% -> 0%
where the time goes in v1:
time: 656 us; the launch traced here: 653 us
  waiting for transfers between devices  338 us (52%)
  blocking collectives  271 us (41%)
  matrix products  17.5 us (3%)
  between operations  14 us (2%)
  other arithmetic  7.18 us (1%)
    pmax x2, blocking collectives, log_total(): top = lax.pmax(local_top, 'vert')  130 us
    psum x2, blocking collectives, log_total(): total = lax.psum(jnp.sum(jnp.exp(values - top[..., None]), axis=-1), 'vert')  128 us
    psum x1, waiting for transfers between devices, local(): down = lax.psum(down_part, 'vert') * down_scale  117 us
    psum x1, waiting for transfers between devices, local(): gate, up = lax.psum((gate_part, up_part), 'wa')  89.1 us
    unnamed x7, waiting for transfers between devices  63.7 us
    all_gather x1, waiting for transfers between devices, local(): states = lax.all_gather(reward_states, 'vert', axis=2, tiled=True)  55.9 us
    psum x1, blocking collectives, normalize(): squares = lax.psum(jnp.sum(resid * resid, axis=1), 'wa')  13.7 us
  transfers between devices with their start and end apart: 10, of which 10 were waited for; matrix products, arithmetic and copies ran while one was open for 0% of the time, Pallas kernels for 0%

profile of v1, /device:TPU:1, one launch (start us, length us, event | category | flops | bytes accessed | tf_op | source)
XLA Modules:
  0.0 653.3 jit_solution(2875951833987203796)
XLA Ops:
  7.2 0.0 copy-start
  7.2 0.0 copy-start.3
  7.2 0.0 all-reduce.8.cloned.1.call-start
  7.2 3.9 fusion.17
  11.2 2.0 fusion.18
  13.2 0.0 all-reduce.8.cloned.1.call-update
  13.3 0.0 all-reduce.6.cloned.1.call-start
  13.3 89.1 %all-reduce.8.cloned.1.call-done = (f32[384,896]{1,0:T(8,128)}, f32[384,896]{1,0:T(8,128)}) async-done(((f32[384,896]{1,0:T(8,128)}, f32[384,896]{1,0:T(8,128)}), (f32[384,896]{1,0:T(8,128)}, f32[384,896]{1,0:T(8,128)})) %all-reduce.8.cloned.1.call-update) | async-done | bytes 2752528 | tf_op jit(solution)/shard_map/psum | solution.py:39
  102.5 3.9 fusion.13
  106.4 0.0 all-reduce.6.cloned.1.call-update
  106.5 0.0 reduce-scatter.7.cloned.1.call-start
  106.5 116.9 %all-reduce.6.cloned.1.call-done = f32[384,1024]{1,0:T(8,128)} async-done(((f32[384,1024]{1,0:T(8,128)}), f32[384,1024]{1,0:T(8,128)}) %all-reduce.6.cloned.1.call-update) | async-done | bytes 1572880 | tf_op jit(solution)/shard_map/psum | solution.py:42
  223.4 2.1 multiply_reduce_fusion
  225.4 13.7 %psum.52 = f32[384]{0:T(512)S(1)} all-reduce(f32[384]{0:T(512)S(1)} %multiply_reduce_fusion), channel_id=1, replica_groups=mesh['wa'=8,'vert'=32] {'wa'}, use_global_device_ids=true, to_apply=%region_4.5 | all-reduce | flops 384 | bytes 3072 | tf_op jit(solution)/shard_map/psum | solution.py:17
  239.1 3.0 fusion.9
  242.1 0.0 reduce-scatter.7.cloned.1.call-update
  242.1 0.0 all-gather.2.cloned.1.call-start
  242.2 0.5 all-gather.2.cloned.1.call-update
  242.7 0.0 reduce-scatter.9.cloned.1.call-start
  242.8 33.5 %reduce-scatter.7.cloned.1.call-done = f32[48,500]{1,0:T(8,128)} async-done(((f32[384,500]{1,0:T(8,128)}), f32[48,500]{1,0:T(8,128)}) %reduce-scatter.7.cloned.1.call-update) | async-done | bytes 96016
  276.3 1.0 copy.23
  277.4 1.1 reduce_max.29
  278.5 55.9 %all-gather.2.cloned.1.call-done = bf16[1,384,4096]{2,1,0:T(8,128)(2,1)} async-done(((bf16[1,384,128]{2,1,0:T(8,128)(2,1)}), bf16[1,384,4096]{2,1,0:T(8,128)(2,1)}) %all-gather.2.cloned.1.call-update) | async-done | bytes 3145744 | tf_op jit(solution)/shard_map/all_gather | solution.py:46
  334.3 2.7 fusion
  337.1 0.1 copy-done.2
  337.2 4.6 fusion.16
  341.8 62.3 %all-reduce.1 = (f32[1,384]{1,0:T(1,128)S(1)}, f32[48]{0:T(128)S(1)}) all-reduce(f32[1,384]{1,0:T(1,128)S(1)} %reduce_max.31, f32[48]{0:T(128)S(1)} %reduce_max.29), channel_id=1, replica_groups=mesh['wa'=8,'vert'=32] {'vert'}, use_global_device_ids=true, to_apply=%region_12.13 | all-reduce | flops 432 | bytes 3456 | tf_op jit(solution)/shard_map/pmax | solution.py:11
  404.1 0.2 exponential_reduce_fusion
  404.3 0.1 exponential_reduce_fusion.2
  404.4 65.2 %all-reduce = (f32[1,384]{1,0:T(1,128)S(1)}, f32[48]{0:T(128)S(1)}) all-reduce(f32[1,384]{1,0:T(1,128)S(1)} %reduce_sum.64, f32[48]{0:T(128)S(1)} %exponential_reduce_fusion.2), channel_id=1, replica_groups=mesh['wa'=8,'vert'=32] {'vert'}, use_global_device_ids=true, to_apply=%region_14.15 | all-reduce | flops 432 | bytes 3456 | tf_op jit(solution)/shard_map/psum | solution.py:12
  469.6 0.1 subtract_multiply_fusion
  469.7 1.2 copy.24
  470.9 0.0 reduce-scatter.9.cloned.1.call-update
  471.0 29.6 %reduce-scatter.9.cloned.1.call-done = f32[48,500]{1,0:T(8,128)} async-done(((f32[384,500]{1,0:T(8,128)}), f32[48,500]{1,0:T(8,128)}) %reduce-scatter.9.cloned.1.call-update) | async-done | bytes 96016
  500.5 1.0 copy.25
  501.6 0.1 fusion.15
  501.7 67.5 %pmax.23 = f32[48]{0:T(128)S(1)} all-reduce(f32[48]{0:T(128)S(1)} %get-tuple-element.14), channel_id=1, replica_groups=mesh['wa'=8,'vert'=32] {'vert'}, use_global_device_ids=true, to_apply=%region_17.18 | all-reduce | flops 48 | bytes 384 | tf_op jit(solution)/shard_map/pmax | solution.py:11
  569.2 0.1 exponential_reduce_fusion.1
  569.3 62.7 %psum.55 = f32[48]{0:T(128)S(1)} all-reduce(f32[48]{0:T(128)S(1)} %exponential_reduce_fusion.1), channel_id=1, replica_groups=mesh['wa'=8,'vert'=32] {'vert'}, use_global_device_ids=true, to_apply=%region_19.20 | all-reduce | flops 48 | bytes 384 | tf_op jit(solution)/shard_map/psum | solution.py:12
  632.0 0.2 select_reduce_fusion
  632.1 0.7 collective-permute-start
  632.8 0.8 collective-permute-done
  633.7 2.4 collective-permute-done.1
  636.1 3.9 collective-permute-done.2
  640.0 2.4 collective-permute-done.3
  642.4 0.8 copy.20
  643.1 3.1 collective-permute-done.4
  646.2 0.5 add.93
  (43 shorter events, 0.2 us)
Async XLA Ops:
  7.2 95.3 %copy-start = (bf16[896,1024]{1,0:T(8,128)(2,1)S(1)}, bf16[896,1024]{1,0:T(8,128)(2,1)}, u32[]{:S(2)}) copy-start(bf16[896,1024]{1,0:T(8,128)(2,1)} %param.19) | copy-start | bytes 5505028
  7.2 4.0 copy-start.3
  7.2 95.3 %all-reduce.8.cloned.1.call-start = ((), (), s32[]{:S(2)}) async-start(), calls=%async_computation.6 | async-start | bytes 5505024 | tf_op jit(solution)/shard_map/psum | solution.py:39
  7.2 4.0 copy-start.10
  13.2 89.2 %copy-start.12 = (f32[896]{0:T(1024)S(1)}, f32[896]{0:T(1024)}, u32[]{:S(2)}) copy-start(f32[896]{0:T(1024)} %param.18) | copy-start | bytes 10756
  13.2 89.2 %copy-start.13 = (f32[896]{0:T(1024)S(1)}, f32[896]{0:T(1024)}, u32[]{:S(2)}) copy-start(f32[896]{0:T(1024)} %param.17) | copy-start | bytes 10756
  13.3 210.1 %all-reduce.6.cloned.1.call-start = ((), (), s32[]{:S(2)}) async-start(), calls=%async_computation.2 | async-start | bytes 3145728 | tf_op jit(solution)/shard_map/psum | solution.py:42
  106.4 116.9 %copy-start.6 = (f32[1024]{0:T(1024)S(1)}, f32[1024]{0:T(1024)}, u32[]{:S(2)}) copy-start(f32[1024]{0:T(1024)} %param.20) | copy-start | bytes 12292
  106.4 132.7 %copy-start.7 = (f32[1024]{0:T(1024)S(1)}, f32[1024]{0:T(1024)}, u32[]{:S(2)}) copy-start(f32[1024]{0:T(1024)} %param.21) | copy-start | bytes 12292
  106.5 169.9 %reduce-scatter.7.cloned.1.call-start = ((), (), s32[]{:S(2)}) async-start(), calls=%async_computation.4 | async-start | bytes 884736
  223.4 15.8 %copy-start.1 = (f32[384,1024]{1,0:T(8,128)S(1)}, f32[384,1024]{1,0:T(8,128)}, u32[]{:S(2)}) copy-start(f32[384,1024]{1,0:T(8,128)} %all-reduce.6.cloned.1.call-done) | copy-start | bytes 4718596
  239.1 3.6 copy-start.8
  242.1 92.2 %all-gather.2.cloned.1.call-start = ((), (), s32[]{:S(2)}) async-start(), calls=%async_computation.3 | async-start | bytes 3244032 | tf_op jit(solution)/shard_map/all_gather | solution.py:46
  242.7 257.8 %reduce-scatter.9.cloned.1.call-start = ((), (), s32[]{:S(2)}) async-start(), calls=%async_computation.5 | async-start | bytes 884736
  277.3 126.9 %copy-start.4 = (f32[48,500]{0,1:T(8,128)}, f32[48,500]{0,1:T(8,128)S(1)}, u32[]{:S(2)}) copy-start(f32[48,500]{0,1:T(8,128)S(1)} %copy.23) | copy-start | bytes 288004
  277.4 59.7 %copy-start.11 = (f32[1,4096]{1,0:T(1,128)S(1)}, f32[1,4096]{1,0:T(1,128)}, u32[]{:S(2)}) copy-start(f32[1,4096]{1,0:T(1,128)} %param.24) | copy-start | bytes 49156
  334.3 2.8 copy-start.2
  469.7 31.8 %copy-start.5 = (f32[48,500]{0,1:T(8,128)S(1)}, f32[48,500]{0,1:T(8,128)}, u32[]{:S(2)}) copy-start(f32[48,500]{0,1:T(8,128)} %copy-done.4) | copy-start | bytes 288004
  469.7 162.2 %copy-start.9 = (s32[48]{0:T(128)S(1)}, s32[48]{0:T(128)}, u32[]{:S(2)}) copy-start(s32[48]{0:T(128)} %param.27) | copy-start | bytes 580
  632.1 1.6 collective-permute-start
  633.7 2.4 collective-permute-start.1
  636.1 3.9 collective-permute-start.2
  640.0 2.4 collective-permute-start.3
  642.4 3.9 collective-permute-start.4
Sparse Core Ops, SparseCore 0:
  13.4 89.0 all-reduce.7
  106.6 116.7 all-reduce.5
  242.3 34.0 reduce-scatter.6
  279.0 55.3 all-gather.1
  471.1 29.4 reduce-scatter.8
